TPU v7x, 32 devices: a whole 2x2x4 slice. The times are simulated.
32 devices in a mesh: gx: 16 (over z, y, x), gy: 2 (over core).
Axes of the slice: x: 2, y: 2, z: 4, core: 2. Of those that a mesh axis runs over, the one named last changes fastest.
Arguments:
- checkpoints: bfloat16 [4, 27, 64, 16, 128], P(None, None, 'gx', 'gy'), may hold values from 0 to 1, as said below
- step_ckpt: int32 [3], replicated, may hold values from 0 to 3, as said below
- solid_mask: int32 [64, 16, 128], P('gx', 'gy'), may hold values from 0 to 1, as said below
- omega: float32 [64, 16, 128], P('gx', 'gy'), may hold values from 0.7 to 1.9
- adjoint_init: float32 [27, 64, 16, 128], P(None, 'gx', 'gy'), may hold values from -150 to 150
Outputs:
- adjoint: float32 [27, 64, 16, 128], P(None, 'gx', 'gy')
- sensitivity: float32 [64, 16, 128], P('gx', 'gy')
- growth: float32 [3], replicated
Inputs may be any that keep to these rules, and one draw needn't show every extreme that they name: `checkpoints`: positive populations, each checkpoint near equilibrium at low Mach number. `step_ckpt`: distinct checkpoint numbers; the first and the last checkpoint are always among them. `solid_mask`: the cells of one solid sphere are 1, all others 0.
All inputs are finite; a program needn't handle non-finite values.
Results may differ from a plain program's by a relative error of at most 0.00075.
Values sent between devices are 32-bit elements; how exact they have to be, the bound alone decides.
A program may use at most 64 MiB of HBM per device.

v0:
```python
import jax
import jax.numpy as jnp
import numpy as np
from jax import lax
from jax.sharding import PartitionSpec as P

STEPS = 3


DIRECTIONS = np.array(
    [[a, b, c] for a in (-1, 0, 1) for b in (-1, 0, 1) for c in (-1, 0, 1)], dtype=np.float32
)
WEIGHTS = np.array([8.0 / 27.0, 2.0 / 27.0, 1.0 / 54.0, 1.0 / 216.0], dtype=np.float32)[
    np.sum(np.abs(DIRECTIONS), axis=1).astype(np.int32)
]


def extended_2(cells, sides, width):
    for axis, dim in sides:
        count = lax.axis_size(axis)
        head = lax.slice_in_dim(cells, 0, width, axis=dim)
        tail = lax.slice_in_dim(cells, cells.shape[dim] - width, cells.shape[dim], axis=dim)
        cells = jnp.concatenate(
            [
                lax.ppermute(tail, axis, [(i, (i + 1) % count) for i in range(count)]),
                cells,
                lax.ppermute(head, axis, [((i + 1) % count, i) for i in range(count)]),
            ],
            axis=dim,
        )
    return cells


def column(values):
    return jnp.asarray(values, jnp.float32).reshape(27, 1, 1, 1)


def extended(field):
    return extended_2(field, (("gx", 1), ("gy", 2)), 1)


def pulled_field(field):
    cells_x, cells_y = (field.shape[1], field.shape[2])
    outer = extended(field)
    pieces = []
    for index in range(27):
        step_x, step_y, step_z = (int(v) for v in DIRECTIONS[index])
        piece = outer[index, 1 + step_x : 1 + step_x + cells_x, 1 + step_y : 1 + step_y + cells_y]
        pieces.append(jnp.roll(piece, -step_z, axis=2))
    return jnp.stack(pieces)


def adjoint_step(pulled, base, omega, fluid):
    rho = jnp.sum(base, axis=0)
    speeds = []
    for axis_num in range(3):
        speeds.append(jnp.sum(column(DIRECTIONS[:, axis_num]) * base, axis=0) / rho)
    along = (
        column(DIRECTIONS[:, 0]) * speeds[0]
        + column(DIRECTIONS[:, 1]) * speeds[1]
        + column(DIRECTIONS[:, 2]) * speeds[2]
    )
    square = speeds[0] * speeds[0] + speeds[1] * speeds[1] + speeds[2] * speeds[2]
    feq = column(WEIGHTS) * rho * (1.0 + 3.0 * along + 4.5 * along * along - 1.5 * square)
    scalar_part = jnp.sum(pulled * feq, axis=0) / rho
    weighted = pulled * column(WEIGHTS)
    plain_sum = jnp.sum(weighted, axis=0)
    total = scalar_part
    for axis_num in range(3):
        dirs = column(DIRECTIONS[:, axis_num])
        vector_part = (
            3.0 * jnp.sum(weighted * dirs * (1.0 + 3.0 * along), axis=0)
            - 3.0 * speeds[axis_num] * plain_sum
        )
        total = total + (dirs - speeds[axis_num]) * vector_part
    fluid_result = (1.0 - omega) * pulled + omega * total
    previous = jnp.where(fluid, fluid_result, pulled[::-1])
    term = jnp.where(fluid, 3.0 * omega * omega * jnp.sum(pulled * (base - feq), axis=0), 0.0)
    return (previous, term)


def body(checkpoints, step_ckpt, solid_mask, omega, adjoint_init):
    fluid = solid_mask == 0
    count = float(adjoint_init.size * lax.axis_size("gx") * lax.axis_size("gy"))
    field = adjoint_init
    sensitivity = jnp.zeros(omega.shape, jnp.float32)
    local_sums = []
    terms = []
    for step in range(STEPS):
        base = lax.dynamic_index_in_dim(checkpoints, step_ckpt[step], 0, keepdims=False).astype(
            jnp.float32
        )
        previous, term = adjoint_step(pulled_field(field), base, omega, fluid)
        terms.append(term)
        local_sums.append(jnp.sum(previous * previous))
        field = previous
    totals = lax.psum(jnp.stack(local_sums), ("gx", "gy"))
    product = jnp.float32(1.0)
    factors = []
    for step in range(STEPS):
        sensitivity = sensitivity + terms[step] / product
        factor = jnp.sqrt(totals[step] / (product * product) / count + 1e-06)
        factors.append(factor)
        product = product * factor
    return (field / product, sensitivity, jnp.stack(factors))


def solution(mesh):
    in_specs = (
        P(None, None, "gx", "gy", None),
        P(),
        P("gx", "gy", None),
        P("gx", "gy", None),
        P(None, "gx", "gy", None),
    )
    out_specs = (P(None, "gx", "gy", None), P("gx", "gy", None), P())
    return jax.shard_map(body, mesh=mesh, in_specs=in_specs, out_specs=out_specs, check_vma=False)
```

profile of v0, /device:TPU:0, one launch (start us, length us, event | category | flops | bytes accessed | tf_op | source)
XLA Modules:
  0.0 103.8 jit_solution(3780960151576092785)
XLA Ops:
  0.6 1.0 %fusion.49 = (f32[27,1,8,128]{3,2,1,0:T(8,128)S(1)}, f32[27,1,8,128]{3,2,1,0:T(8,128)S(1)}) fusion(f32[27,4,8,128]{3,2,1,0:T(8,128)} %param.42), kind=kLoop, calls=%fused_computation.313 | loop fusion | bytes 442368 | tf_op jit(solution)/shard_map/slice | solution.py:21
  1.7 3.0 %collective-permute-start = (f32[27,1,8,128]{3,2,1,0:T(8,128)S(1)}, f32[27,1,8,128]{3,2,1,0:T(8,128)S(1)}, u32[]{:S(2)}, u32[]{:S(2)}) collective-permute-start(f32[27,1,8,128]{3,2,1,0:T(8,128)S(1)} %get-tuple-element.140), channel_id=1, source_target_pairs={{0,2},{2,4},{4,6},{6,8},{8,10},{10,12},{12,14},{14,16},{16,18},{18... | collective-permute-start | bytes 331784 | tf_op jit(solution)/shard_map/ppermute | solution.py:25
  4.7 4.1 %collective-permute-start.1 = (f32[27,1,8,128]{3,2,1,0:T(8,128)S(1)}, f32[27,1,8,128]{3,2,1,0:T(8,128)S(1)}, u32[]{:S(2)}, u32[]{:S(2)}) collective-permute-start(f32[27,1,8,128]{3,2,1,0:T(8,128)S(1)} %get-tuple-element.139), channel_id=1, source_target_pairs={{2,0},{4,2},{6,4},{8,6},{10,8},{12,10},{14,12},{16,14},{18,16},{20... | collective-permute-start | bytes 331784 | tf_op jit(solution)/shard_map/ppermute | solution.py:27
  8.7 0.7 slice_bitcast_fusion.9
  9.5 1.4 %fusion.51 = (s32[1]{0:T(128)}, s32[1]{0:T(128)}, s32[1]{0:T(128)}) fusion(s32[3]{0:T(128)} %param.39), kind=kLoop, calls=%fused_computation.315 | loop fusion | bytes 24 | tf_op jit(solution)/shard_map/slice | solution.py:90
  16.7 1.3 %convert_reduce_fusion = (f32[4,8,128]{2,1,0:T(8,128)S(1)}, f32[4,8,128]{2,1,0:T(8,128)S(1)}, f32[4,8,128]{2,1,0:T(8,128)S(1)}) fusion(bf16[4,27,4,8,128]{4,3,2,1,0:T(8,128)(2,1)} %param.38, s32[]{:T(128)S(6)} %select_n.34, s32[]{:T(128)S(6)} %select_n.30, s32[]{:T(128)S(6)} %select_n.32), kind=kLoop, calls=%fused_computation.4 | loop fusion | flops 651264 | bytes 712716 | tf_op jit(solution)/shard_map/reduce_sum | solution.py:54
  18.3 0.7 copy-done.3
  20.1 0.6 collective-permute-done.2
  23.3 0.7 copy-done.7
  24.5 0.7 copy-done.2
  25.2 1.0 multiply_reduce_fusion.2
  26.3 5.7 %collective-permute-start.5 = (f32[27,1,8,128]{3,2,1,0:T(8,128)S(1)}, f32[27,1,8,128]{3,2,1,0:T(8,128)S(1)}, u32[]{:S(2)}, u32[]{:S(2)}) collective-permute-start(f32[27,1,8,128]{3,2,1,0:T(8,128)S(1)} %get-tuple-element.132), channel_id=1, source_target_pairs={{2,0},{4,2},{6,4},{8,6},{10,8},{12,10},{14,12},{16,14},{18,16},{20... | collective-permute-start | bytes 331784 | tf_op jit(solution)/shard_map/ppermute | solution.py:27
  31.9 3.2 %collective-permute-done.4 = f32[27,1,8,128]{3,2,1,0:T(8,128)S(1)} collective-permute-done((f32[27,1,8,128]{3,2,1,0:T(8,128)S(1)}, f32[27,1,8,128]{3,2,1,0:T(8,128)S(1)}, u32[]{:S(2)}, u32[]{:S(2)}) %collective-permute-start.4) | collective-permute-done | bytes 110624 | tf_op jit(solution)/shard_map/ppermute | solution.py:25
  36.5 0.7 collective-permute-done.7
  40.2 0.7 fusion.21
  40.9 1.0 multiply_reduce_fusion.1
  42.0 5.6 %collective-permute-start.9 = (f32[27,1,8,128]{3,2,1,0:T(8,128)S(1)}, f32[27,1,8,128]{3,2,1,0:T(8,128)S(1)}, u32[]{:S(2)}, u32[]{:S(2)}) collective-permute-start(f32[27,1,8,128]{3,2,1,0:T(8,128)S(1)} %get-tuple-element.128), channel_id=1, source_target_pairs={{2,0},{4,2},{6,4},{8,6},{10,8},{12,10},{14,12},{16,14},{18,16},{20... | collective-permute-start | bytes 331784 | tf_op jit(solution)/shard_map/ppermute | solution.py:27
  47.6 3.3 %collective-permute-done.8 = f32[27,1,8,128]{3,2,1,0:T(8,128)S(1)} collective-permute-done((f32[27,1,8,128]{3,2,1,0:T(8,128)S(1)}, f32[27,1,8,128]{3,2,1,0:T(8,128)S(1)}, u32[]{:S(2)}, u32[]{:S(2)}) %collective-permute-start.8) | collective-permute-done | bytes 110624 | tf_op jit(solution)/shard_map/ppermute | solution.py:25
  51.7 0.7 collective-permute-done.10
  55.4 0.9 fusion.16
  56.3 1.0 multiply_reduce_fusion
  57.3 2.0 %pad_maximum_fusion.25 = f32[3]{0:T(128)S(1)} fusion(f32[1]{0:T(128)} %bitcast.116, f32[1]{0:T(128)} %bitcast.115, f32[1]{0:T(128)} %bitcast.114), kind=kLoop, calls=%fused_computation.307 | loop fusion | flops 6 | bytes 24 | tf_op jit(solution)/shard_map/stack | solution.py:97
  59.3 39.7 %psum.7 = f32[3]{0:T(128)S(1)} all-reduce(f32[3]{0:T(128)S(1)} %pad_maximum_fusion.25), channel_id=1, replica_groups=mesh['gx'=16,'gy'=2] {'gx','gy'}, use_global_device_ids=true, to_apply=%region_30.31 | all-reduce | flops 3 | bytes 24 | tf_op jit(solution)/shard_map/psum | solution.py:97
  102.3 0.8 broadcast_divide_fusion
  (202 shorter events, 14.4 us)
Async XLA Ops:
  0.6 17.3 %copy-start = (bf16[4,27,4,8,128]{4,3,2,1,0:T(8,128)(2,1)S(1)}, bf16[4,27,4,8,128]{4,3,2,1,0:T(8,128)(2,1)}, u32[]{:S(2)}) copy-start(bf16[4,27,4,8,128]{4,3,2,1,0:T(8,128)(2,1)} %param.38) | copy-start | bytes 2654212
  1.7 17.4 %collective-permute-start = (f32[27,1,8,128]{3,2,1,0:T(8,128)S(1)}, f32[27,1,8,128]{3,2,1,0:T(8,128)S(1)}, u32[]{:S(2)}, u32[]{:S(2)}) collective-permute-start(f32[27,1,8,128]{3,2,1,0:T(8,128)S(1)} %get-tuple-element.140), channel_id=1, source_target_pairs={{0,2},{2,4},{4,6},{6,8},{8,10},{10,12},{12,14},{14,16},{16,18},{18... | collective-permute-start | bytes 331784 | tf_op jit(solution)/shard_map/ppermute | solution.py:25
  4.7 14.5 %collective-permute-start.1 = (f32[27,1,8,128]{3,2,1,0:T(8,128)S(1)}, f32[27,1,8,128]{3,2,1,0:T(8,128)S(1)}, u32[]{:S(2)}, u32[]{:S(2)}) collective-permute-start(f32[27,1,8,128]{3,2,1,0:T(8,128)S(1)} %get-tuple-element.139), channel_id=1, source_target_pairs={{2,0},{4,2},{6,4},{8,6},{10,8},{12,10},{14,12},{16,14},{18,16},{20... | collective-permute-start | bytes 331784 | tf_op jit(solution)/shard_map/ppermute | solution.py:27
  16.6 1.3 %copy-start.4 = (f32[27]{0:T(128)S(1)}, f32[27]{0:T(128)}, u32[]{:S(2)}) copy-start(f32[27]{0:T(128)} %constant.43.clone) | copy-start | bytes 328
  16.7 1.3 %copy-start.5 = (f32[27]{0:T(128)S(1)}, f32[27]{0:T(128)}, u32[]{:S(2)}) copy-start(f32[27]{0:T(128)} %constant.44.clone) | copy-start | bytes 328
  16.7 1.3 %copy-start.6 = (f32[27]{0:T(128)S(1)}, f32[27]{0:T(128)}, u32[]{:S(2)}) copy-start(f32[27]{0:T(128)} %constant.45.clone) | copy-start | bytes 328
  18.0 1.1 %copy-start.1 = (f32[27,4,8,128]{3,2,1,0:T(8,128)S(1)}, f32[27,4,8,128]{3,2,1,0:T(8,128)}, u32[]{:S(2)}) copy-start(f32[27,4,8,128]{3,2,1,0:T(8,128)} %param.42) | copy-start | bytes 1327108
  18.2 0.7 copy-start.3
  19.3 1.3 %collective-permute-start.2 = (f32[27,6,1,128]{3,2,1,0:T(1,128)S(1)}, f32[27,6,1,128]{3,2,1,0:T(1,128)S(1)}, u32[]{:S(2)}, u32[]{:S(2)}) collective-permute-start(f32[27,6,1,128]{3,2,1,0:T(1,128)S(1)} %get-tuple-element.111), channel_id=1, source_target_pairs={{0,1},{1,0},{2,3},{3,2},{4,5},{5,4},{6,7},{7,6},{8,9},{9,8},{10,11... | collective-permute-start | bytes 248840 | tf_op jit(solution)/shard_map/ppermute | solution.py:25
  19.4 1.4 %collective-permute-start.3 = (f32[27,6,1,128]{3,2,1,0:T(1,128)S(1)}, f32[27,6,1,128]{3,2,1,0:T(1,128)S(1)}, u32[]{:S(2)}, u32[]{:S(2)}) collective-permute-start(f32[27,6,1,128]{3,2,1,0:T(1,128)S(1)} %get-tuple-element.110), channel_id=1, source_target_pairs={{1,0},{0,1},{3,2},{2,3},{5,4},{4,5},{7,6},{6,7},{9,8},{8,9},{11,10... | collective-permute-start | bytes 248840 | tf_op jit(solution)/shard_map/ppermute | solution.py:27
  23.3 0.7 copy-start.7
  24.4 0.7 copy-start.2
  26.2 9.0 %collective-permute-start.4 = (f32[27,1,8,128]{3,2,1,0:T(8,128)S(1)}, f32[27,1,8,128]{3,2,1,0:T(8,128)S(1)}, u32[]{:S(2)}, u32[]{:S(2)}) collective-permute-start(f32[27,1,8,128]{3,2,1,0:T(8,128)S(1)} %get-tuple-element.133), channel_id=1, source_target_pairs={{0,2},{2,4},{4,6},{6,8},{8,10},{10,12},{12,14},{14,16},{16,18},{18... | collective-permute-start | bytes 331784 | tf_op jit(solution)/shard_map/ppermute | solution.py:25
  26.3 9.2 %collective-permute-start.5 = (f32[27,1,8,128]{3,2,1,0:T(8,128)S(1)}, f32[27,1,8,128]{3,2,1,0:T(8,128)S(1)}, u32[]{:S(2)}, u32[]{:S(2)}) collective-permute-start(f32[27,1,8,128]{3,2,1,0:T(8,128)S(1)} %get-tuple-element.132), channel_id=1, source_target_pairs={{2,0},{4,2},{6,4},{8,6},{10,8},{12,10},{14,12},{16,14},{18,16},{20... | collective-permute-start | bytes 331784 | tf_op jit(solution)/shard_map/ppermute | solution.py:27
  35.9 1.4 %collective-permute-start.7 = (f32[27,6,1,128]{3,0,2,1:T(8,128)S(1)}, f32[27,6,1,128]{3,0,2,1:T(8,128)S(1)}, u32[]{:S(2)}, u32[]{:S(2)}) collective-permute-start(f32[27,6,1,128]{3,0,2,1:T(8,128)S(1)} %get-tuple-element.64), channel_id=1, source_target_pairs={{1,0},{0,1},{3,2},{2,3},{5,4},{4,5},{7,6},{6,7},{9,8},{8,9},{11,10... | collective-permute-start | bytes 248840 | tf_op jit(solution)/shard_map/ppermute | solution.py:27
  36.0 1.4 %collective-permute-start.6 = (f32[27,6,1,128]{3,0,2,1:T(8,128)S(1)}, f32[27,6,1,128]{3,0,2,1:T(8,128)S(1)}, u32[]{:S(2)}, u32[]{:S(2)}) collective-permute-start(f32[27,6,1,128]{3,0,2,1:T(8,128)S(1)} %get-tuple-element.65), channel_id=1, source_target_pairs={{0,1},{1,0},{2,3},{3,2},{4,5},{5,4},{6,7},{7,6},{8,9},{9,8},{10,11... | collective-permute-start | bytes 248840 | tf_op jit(solution)/shard_map/ppermute | solution.py:25
  41.9 9.0 %collective-permute-start.8 = (f32[27,1,8,128]{3,2,1,0:T(8,128)S(1)}, f32[27,1,8,128]{3,2,1,0:T(8,128)S(1)}, u32[]{:S(2)}, u32[]{:S(2)}) collective-permute-start(f32[27,1,8,128]{3,2,1,0:T(8,128)S(1)} %get-tuple-element.127), channel_id=1, source_target_pairs={{0,2},{2,4},{4,6},{6,8},{8,10},{10,12},{12,14},{14,16},{16,18},{18... | collective-permute-start | bytes 331784 | tf_op jit(solution)/shard_map/ppermute | solution.py:25
  42.0 8.9 %collective-permute-start.9 = (f32[27,1,8,128]{3,2,1,0:T(8,128)S(1)}, f32[27,1,8,128]{3,2,1,0:T(8,128)S(1)}, u32[]{:S(2)}, u32[]{:S(2)}) collective-permute-start(f32[27,1,8,128]{3,2,1,0:T(8,128)S(1)} %get-tuple-element.128), channel_id=1, source_target_pairs={{2,0},{4,2},{6,4},{8,6},{10,8},{12,10},{14,12},{16,14},{18,16},{20... | collective-permute-start | bytes 331784 | tf_op jit(solution)/shard_map/ppermute | solution.py:27
  51.0 1.4 %collective-permute-start.10 = (f32[27,6,1,128]{3,0,2,1:T(8,128)S(1)}, f32[27,6,1,128]{3,0,2,1:T(8,128)S(1)}, u32[]{:S(2)}, u32[]{:S(2)}) collective-permute-start(f32[27,6,1,128]{3,0,2,1:T(8,128)S(1)} %copy.54), channel_id=1, source_target_pairs={{0,1},{1,0},{2,3},{3,2},{4,5},{5,4},{6,7},{7,6},{8,9},{9,8},{10,11... | collective-permute-start | bytes 248840 | tf_op jit(solution)/shard_map/ppermute | solution.py:25
  51.1 1.5 %collective-permute-start.11 = (f32[27,6,1,128]{3,0,2,1:T(8,128)S(1)}, f32[27,6,1,128]{3,0,2,1:T(8,128)S(1)}, u32[]{:S(2)}, u32[]{:S(2)}) collective-permute-start(f32[27,6,1,128]{3,0,2,1:T(8,128)S(1)} %copy.56), channel_id=1, source_target_pairs={{1,0},{0,1},{3,2},{2,3},{5,4},{4,5},{7,6},{6,7},{9,8},{8,9},{11,10... | collective-permute-start | bytes 248840 | tf_op jit(solution)/shard_map/ppermute | solution.py:27
where the time goes:
time: 104 us
  blocking collectives  39.7 us (38%)
  starting transfers between devices  20.2 us (19%)
  other arithmetic  15.1 us (15%)
  local copies, waits for them, and re-layouts  11 us (11%)
  between operations  9.12 us (9%)
  waiting for transfers between devices  8.59 us (8%)
    psum x1, blocking collectives, body(): totals = lax.psum(jnp.stack(local_sums), ('gx', 'gy'))  39.7 us
    ppermute x6, starting transfers between devices, extended_2(): lax.ppermute(head, axis, [((i + 1) % count, i) for i in range(count)])  16.5 us
    ppermute x6, waiting for transfers between devices, extended_2(): lax.ppermute(tail, axis, [(i, (i + 1) % count) for i in range(count)])  7.86 us
    slice x54, local copies, waits for them, and re-layouts, pulled_field(): pieces.append(jnp.roll(piece, -step_z, axis=2))  3.92 us
    unnamed x53, other arithmetic  3.89 us
    ppermute x6, starting transfers between devices, extended_2(): lax.ppermute(tail, axis, [(i, (i + 1) % count) for i in range(count)])  3.74 us
    reduce_sum x3, other arithmetic, body(): local_sums.append(jnp.sum(previous * previous))  2.9 us
    unnamed x25, local copies, waits for them, and re-layouts  2.47 us
  transfers between devices with their start and end apart: 12, of which 6 were waited for; matrix products, arithmetic and copies ran while one was open for 5% of the time, Pallas kernels for 0%

commit v1 on v0

v1 whole, which is shorter than its diff:
```python
import functools

import jax
import jax.numpy as jnp
from jax import lax
from jax.experimental import pallas as pl
from jax.experimental.pallas import tpu as pltpu
from jax.sharding import PartitionSpec as P

MESH = pl.DeviceIdType.MESH
EDGE = 16
CORNERS = ((0, 0), (0, 1), (1, 0), (1, 1))


def three(minus, plain, plus):
    even = plus + minus
    return 4.0 * plain + even, plus - minus, even


def weighted_moments(p):
    along_z = [three(*p[3 * k : 3 * k + 3]) for k in range(9)]
    along_y = []
    for a in range(3):
        rows = along_z[3 * a : 3 * a + 3]
        y0 = three(*[r[0] for r in rows])
        y1 = three(*[r[1] for r in rows])
        y2 = three(*[r[2] for r in rows])
        along_y.append((y0[0], y0[1], y0[2], y1[0], y1[1], y2[0]))
    m, my, myy, mz, myz, mzz = (three(*[r[k] for r in along_y]) for k in range(6))
    return m[0], m[1], my[0], mz[0], m[2], myy[0], mzz[0], my[1], mz[1], myz[0]


def plain_moments(f):
    zs = [(f[3 * k] + f[3 * k + 2] + f[3 * k + 1], f[3 * k + 2] - f[3 * k]) for k in range(9)]
    ys = []
    for a in range(3):
        r = zs[3 * a : 3 * a + 3]
        ys.append((r[0][0] + r[2][0] + r[1][0], r[2][0] - r[0][0], r[0][1] + r[1][1] + r[2][1]))
    total = [ys[0][k] + ys[1][k] + ys[2][k] for k in range(3)]
    return total[0], ys[2][0] - ys[0][0], total[1], total[2]


def kernel(
    steps, nx, ny, nz, ngx, ngy,
    idx_ref, ck_hbm, solid_hbm, omega_hbm, adj_hbm,
    out_ref, sens_ref, growth_ref,
    ck_ref, solid_ref, omega_ref, adj_ref,
    fld, ysend, yrecv, fval, mom, terms, acc_ref, line_y, line_x, own_y, own_x,
    local_sem, send_sem, recv_sem, ysum_send, ysum_recv, xsum_send, xsum_recv,
):
    gx, gy = lax.axis_index("gx"), lax.axis_index("gy")
    plane = 27 * ny

    def gxs(k):
        return lax.rem(gx + (k + ngx), ngx)

    def gys(k):
        return lax.rem(gy + (k + ngy), ngy)

    loads = [
        pltpu.make_async_copy(src, dst, local_sem.at[n])
        for n, (src, dst) in enumerate(
            ((adj_hbm, adj_ref), (ck_hbm, ck_ref), (solid_hbm, solid_ref), (omega_hbm, omega_ref))
        )
    ]
    for copy in loads:
        copy.start()

    barrier = pltpu.get_barrier_semaphore()
    greeted = (
        [(gxs(k), gy) for k in range(1, ngx)]
        + [(gx, gys(k)) for k in range(1, ngy)]
        + [(gxs(a), gys(b)) for a in (-1, 1) for b in (-1, 1)]
    )
    for device in greeted:
        pl.semaphore_signal(barrier, inc=1, device_id=device, device_id_type=MESH)

    loads[0].wait()
    for x in range(nx):
        for i in range(27):
            fld[0, pl.ds((x + 1) * plane + i * ny, ny), :] = adj_ref[i, x]

    def pack(s):
        for x in range(nx):
            for d in (0, 1):
                row = 0 if d == 1 else ny - 1
                for a in range(3):
                    start = (x + 1) * plane + (9 * a + 6 * d) * ny + row
                    ysend[s, d, pl.ds(x * EDGE + 4 * a, 3), :] = fld[s, pl.ds(start, 3, stride=ny), :]

    def copies(s):
        todo = [
            (fld.at[s, pl.ds(nx * plane, 9 * ny), :], fld.at[s, pl.ds(0, 9 * ny), :], (gxs(1), gy)),
            (
                fld.at[s, pl.ds(plane + 18 * ny, 9 * ny), :],
                fld.at[s, pl.ds((nx + 1) * plane + 18 * ny, 9 * ny), :],
                (gxs(-1), gy),
            ),
        ]
        for d in (0, 1):
            todo.append(
                (ysend.at[s, d], yrecv.at[s, d, pl.ds(EDGE, nx * EDGE), :], (gx, gys(1 - 2 * d)))
            )
        for a, d in CORNERS:
            src = 8 if a else (nx - 1) * EDGE
            dst = (nx + 1) * EDGE + 8 if a else 0
            todo.append(
                (
                    ysend.at[s, d, pl.ds(src, 8), :],
                    yrecv.at[s, d, pl.ds(dst, 8), :],
                    (gxs(1 - 2 * a), gys(1 - 2 * d)),
                )
            )
        return [
            pltpu.make_async_remote_copy(
                src_ref=src,
                dst_ref=dst,
                send_sem=send_sem.at[s, n],
                recv_sem=recv_sem.at[s, n],
                device_id=device,
                device_id_type=MESH,
            )
            for n, (src, dst, device) in enumerate(todo)
        ]

    def base_moments(s):
        which = idx_ref[s]

        def pair(k, _):
            rows = pl.ds(pl.multiple_of(k * 2 * ny, 2 * ny), 2 * ny)
            f = [ck_ref[which, i, rows, :].astype(jnp.float32) for i in range(27)]
            for i in range(27):
                fval[s, i, rows, :] = f[i]
            rho, jx, jy, jz = plain_moments(f)
            inv = 1.0 / rho
            for n, value in enumerate((rho, jx * inv, jy * inv, jz * inv)):
                mom[s, n, rows, :] = value
            return 0

        lax.fori_loop(0, nx // 2, pair, 0)

    lane_row = lax.broadcasted_iota(jnp.int32, (ny, nz), 0)
    first, last = lane_row == 0, lane_row == ny - 1

    def step_plane(s, x):
        p = []
        for i in range(27):
            a, b, c = i // 9, i // 3 % 3, i % 3
            start = pl.multiple_of((x + a) * plane + i * ny, ny)
            tile = fld[s, pl.ds(start, ny), :]
            if b != 1:
                edge = yrecv[s, b // 2, pl.ds((x + a) * EDGE + 4 * a + c, 1), :]
                tile = jnp.where(first if b == 2 else last, jnp.broadcast_to(edge, (ny, nz)), tile)
                tile = pltpu.roll(tile, ny - 1 if b == 2 else 1, 0)
            if c != 1:
                tile = pltpu.roll(tile, nz - 1 if c == 2 else 1, 1)
            p.append(tile)
        rows = pl.ds(pl.multiple_of(x * ny, ny), ny)
        rho, ux, uy, uz = (mom[s, n, rows, :] for n in range(4))
        omega = omega_ref[rows, :]
        fluid = solid_ref[rows, :] == 0
        m0, mx, my, mz, mxx, myy, mzz, mxy, mxz, myz = weighted_moments(p)
        vx = mxx * ux + mxy * uy + mxz * uz
        vy = mxy * ux + myy * uy + myz * uz
        vz = mxz * ux + myz * uy + mzz * uz
        square = ux * ux + uy * uy + uz * uz
        um = ux * mx + uy * my + uz * mz
        uv = ux * vx + uy * vy + uz * vz
        scale = 1.0 / 216.0
        total = scale * (m0 * (1.0 - 1.5 * square) + 3.0 * um + 4.5 * uv)
        gxv = scale * (3.0 * (mx - ux * m0) + 9.0 * vx)
        gyv = scale * (3.0 * (my - uy * m0) + 9.0 * vy)
        gzv = scale * (3.0 * (mz - uz * m0) + 9.0 * vz)
        base = omega * (total - (ux * gxv + uy * gyv + uz * gzv))
        wx, wy, wz = omega * gxv, omega * gyv, omega * gzv
        keep = 1.0 - omega
        square_sum = None
        for a in range(3):
            ta = base if a == 1 else (base + wx if a == 2 else base - wx)
            for b in range(3):
                tb = ta if b == 1 else (ta + wy if b == 2 else ta - wy)
                for c in range(3):
                    tc = tb if c == 1 else (tb + wz if c == 2 else tb - wz)
                    i = 9 * a + 3 * b + c
                    value = jnp.where(fluid, keep * p[i] + tc, p[26 - i])
                    start = pl.multiple_of((x + 1) * plane + i * ny, ny)
                    fld[s + 1, pl.ds(start, ny), :] = value
                    square_sum = value * value if square_sum is None else square_sum + value * value
        pf = None
        for i in range(27):
            product = p[i] * fval[s, i, rows, :]
            pf = product if pf is None else pf + product
        terms[s, rows, :] = jnp.where(fluid, 3.0 * omega * omega * (pf - rho * total), 0.0)
        acc_ref[s] += square_sum

    acc_ref[...] = jnp.zeros_like(acc_ref)
    pack(0)
    pl.semaphore_wait(barrier, len(greeted))

    sent = []
    for s in range(steps):
        moving = copies(s)
        sent += moving
        for copy in moving:
            copy.start()
        if s == 0:
            for copy in loads[1:]:
                copy.wait()
        base_moments(s)
        for copy in moving[2:4]:
            copy.wait_recv()
        lax.fori_loop(1, nx - 1, lambda x, _, s=s: (step_plane(s, x), 0)[1], 0)
        for copy in moving[:2] + moving[4:]:
            copy.wait_recv()
        lax.fori_loop(0, 2, lambda t, _, s=s: (step_plane(s, t * (nx - 1)), 0)[1], 0)
        if s + 1 < steps:
            pack(s + 1)

    lane = lax.broadcasted_iota(jnp.int32, (1, nz), 1)
    row = jnp.zeros((1, nz), jnp.float32)
    for s in range(steps):
        value = jnp.sum(jnp.sum(acc_ref[s], axis=0, keepdims=True), axis=1, keepdims=True)
        row = row + jnp.where(lane == s, value, 0.0)

    def spread(row, own, line, me, count, send, recv, place):
        own[0] = row
        copies = [
            pltpu.make_async_remote_copy(
                src_ref=own.at[0],
                dst_ref=line.at[k - 1],
                send_sem=send.at[k - 1],
                recv_sem=recv.at[k - 1],
                device_id=place(k),
                device_id_type=MESH,
            )
            for k in range(1, count)
        ]
        for copy in copies:
            copy.start()
        for copy in copies:
            copy.wait_recv()
        for k in range(count - 1):
            row = row + line[k]
        return row, copies

    row, more = spread(row, own_y, line_y, gy, ngy, ysum_send, ysum_recv, lambda k: (gx, gys(k)))
    sent += more
    row, more = spread(row, own_x, line_x, gx, ngx, xsum_send, xsum_recv, lambda k: (gxs(k), gy))
    sent += more

    inverse = jnp.ones((1, nz), jnp.float32)
    sens = jnp.zeros((nx * ny, nz), jnp.float32)
    count = float(27 * nx * ny * nz * ngx * ngy)
    for s in range(steps):
        sens = sens + terms[s] * inverse
        total = jnp.sum(jnp.where(lane == s, row, 0.0), axis=1, keepdims=True)
        total = jnp.broadcast_to(total, (1, nz))
        factor = jnp.sqrt(total * (inverse * inverse) * (1.0 / count) + 1e-06)
        inverse = inverse / factor
        growth_ref[pl.ds(s, 1), :] = factor
    sens_ref[...] = sens
    for x in range(nx):
        for i in range(27):
            out_ref[i, x] = fld[steps, pl.ds((x + 1) * plane + i * ny, ny), :] * inverse
    for copy in sent:
        copy.wait_send()


def body(checkpoints, step_ckpt, solid_mask, omega, adjoint_init):
    nck, _, nx, ny, nz = checkpoints.shape
    steps = step_ckpt.shape[0]
    ngx, ngy = lax.axis_size("gx"), lax.axis_size("gy")
    f32 = jnp.float32
    hbm = pl.BlockSpec(memory_space=pltpu.HBM)
    vmem = pl.BlockSpec(memory_space=pltpu.VMEM)
    dma = pltpu.SemaphoreType.DMA
    rows = (nx + 2) * 27 * ny
    out, sens, growth = pl.pallas_call(
        functools.partial(kernel, steps, nx, ny, nz, ngx, ngy),
        out_shape=(
            jax.ShapeDtypeStruct(adjoint_init.shape, f32),
            jax.ShapeDtypeStruct((nx * ny, nz), f32),
            jax.ShapeDtypeStruct((steps, nz), f32),
        ),
        in_specs=[pl.BlockSpec(memory_space=pltpu.SMEM), hbm, hbm, hbm, hbm],
        out_specs=(vmem, vmem, vmem),
        scratch_shapes=[
            pltpu.VMEM((nck, 27, nx * ny, nz), checkpoints.dtype),
            pltpu.VMEM((nx * ny, nz), jnp.int32),
            pltpu.VMEM((nx * ny, nz), f32),
            pltpu.VMEM(adjoint_init.shape, f32),
            pltpu.VMEM((steps + 1, rows, nz), f32),
            pltpu.VMEM((steps, 2, nx * EDGE, nz), f32),
            pltpu.VMEM((steps, 2, (nx + 2) * EDGE, nz), f32),
            pltpu.VMEM((steps, 27, nx * ny, nz), f32),
            pltpu.VMEM((steps, 4, nx * ny, nz), f32),
            pltpu.VMEM((steps, nx * ny, nz), f32),
            pltpu.VMEM((steps, ny, nz), f32),
            pltpu.VMEM((max(ngy - 1, 1), 1, nz), f32),
            pltpu.VMEM((max(ngx - 1, 1), 1, nz), f32),
            pltpu.VMEM((1, 1, nz), f32),
            pltpu.VMEM((1, 1, nz), f32),
            dma((4,)),
            dma((steps, 8)),
            dma((steps, 8)),
            dma((max(ngy - 1, 1),)),
            dma((max(ngy - 1, 1),)),
            dma((max(ngx - 1, 1),)),
            dma((max(ngx - 1, 1),)),
        ],
        compiler_params=pltpu.CompilerParams(
            collective_id=0, has_side_effects=True, vmem_limit_bytes=60 * 1024 * 1024
        ),
        cost_estimate=pl.CostEstimate(flops=10**7, bytes_accessed=2 * 10**6, transcendentals=0),
    )(
        step_ckpt,
        checkpoints.reshape(nck, 27, nx * ny, nz),
        solid_mask.reshape(nx * ny, nz),
        omega.reshape(nx * ny, nz),
        adjoint_init,
    )
    return out, sens.reshape(omega.shape), growth[:, 0]


def solution(mesh):
    in_specs = (
        P(None, None, "gx", "gy", None),
        P(),
        P("gx", "gy", None),
        P("gx", "gy", None),
        P(None, "gx", "gy", None),
    )
    out_specs = (P(None, "gx", "gy", None), P("gx", "gy", None), P())
    return jax.shard_map(body, mesh=mesh, in_specs=in_specs, out_specs=out_specs, check_vma=False)
```

time: 104 us -> 34.3 us (0.33)
  blocking collectives: 39.7 us -> 0 us
  Pallas kernels: 0 us -> 29.7 us
  starting transfers between devices: 20.2 us -> 0 us
  other arithmetic: 15.1 us -> 0 us
  waiting for transfers between devices: 8.59 us -> 0 us
  between operations: 9.12 us -> 0.65 us
  local copies, waits for them, and re-layouts: 11 us -> 3.72 us
    psum x1 -> x0, blocking collectives: 39.7 us -> none  [body(): totals = lax.psum(jnp.stack(local_sums), ('gx', 'gy'))]
    pallas_call x0 -> x1, Pallas kernels: none -> 29.7 us  [body(): pl.pallas_call(functools.partial(kernel, steps, nx, ny, nz, ngx, ngy), ou...]
    ppermute x12 -> x0, starting transfers between devices: 20.2 us -> none  [the longest x6 16.5 us: extended_2(): lax.ppermute(head, axis, [((i + 1) % count, i) for i in range(count)])]
    ppermute x12 -> x0, waiting for transfers between devices: 8.59 us -> none  [the longest x6 7.86 us: extended_2(): lax.ppermute(tail, axis, [(i, (i + 1) % count) for i in range(count)])]
    slice x63 -> x1, local copies, waits for them, and re-layouts: 7.08 us -> 0.63 us  [body(): return (out, sens.reshape(omega.shape), growth[:, 0])]
    reduce_sum x8 -> x0, other arithmetic: 6.4 us -> none  [the longest x3 2.9 us: body(): local_sums.append(jnp.sum(previous * previous))]
    unnamed x53 -> x0, other arithmetic: 3.89 us -> none
    another operation x5 -> x0, other arithmetic: 2.83 us -> none  [the longest x1 2.01 us: body(): totals = lax.psum(jnp.stack(local_sums), ('gx', 'gy'))]
  transfers between devices with their start and end apart: 12 -> 0, of which waited for: 6 -> 0; matrix products, arithmetic and copies ran while one was open for 5% -> 0% of each run, Pallas kernels for 0% -> 0%
where the time goes in v1:
time: 34.3 us; the launch traced here: 34.1 us
  Pallas kernels  29.7 us (87%)
  local copies, waits for them, and re-layouts  3.72 us (11%)
  between operations  0.65 us (2%)
    pallas_call x1, Pallas kernels, body(): pl.pallas_call(functools.partial(kernel, steps, nx, ny, nz, ngx, ngy), ou...  29.7 us
    unnamed x6, local copies, waits for them, and re-layouts  3.1 us

profile of v1, /device:TPU:0, one launch (start us, length us, event | category | flops | bytes accessed | tf_op | source)
XLA Modules:
  0.0 34.1 jit_solution(16417289657982468511)
XLA Ops:
  0.6 29.7 %shard_map.76 = (f32[27,4,8,128]{3,2,1,0:T(8,128)}, f32[32,128]{1,0:T(8,128)}, f32[3,128]{1,0:T(4,128)}) custom-call(s32[3]{0:T(128)} %idx_ref.1, bf16[4,27,32,128]{3,2,1,0:T(8,128)(2,1)} %bitcast.4, s32[32,128]{1,0:T(8,128)} %bitcast.5, f32[32,128]{1,0:T(8,128)} %bitcast.6, f32[27,4,8,128]{3,2,1,0:T(8,128)} %adj_hbm.1), custom_call_target="tpu_custom_call" | custom-call | flops 10000000 | bytes 2000000 | tf_op jit(solution)/shard_map/pallas_call | solution.py:278
  30.4 0.0 copy-start.1
  30.4 0.7 %copy-done.1 = f32[3,128]{1,0:T(4,128)S(1)} copy-done((f32[3,128]{1,0:T(4,128)S(1)}, f32[3,128]{1,0:T(4,128)}, u32[]{:S(2)}) %copy-start.1) | copy-done | bytes 1560
  31.0 0.6 %slice_reduce_fusion = f32[3]{0:T(128)} fusion(f32[3,128]{1,0:T(4,128)S(1)} %copy-done.1), kind=kLoop, calls=%fused_computation | loop fusion | bytes 24 | tf_op jit(solution)/shard_map/slice | solution.py:322
  31.7 0.0 copy-start
  31.7 1.8 %copy.10 = f32[27,4,8,128]{3,2,1,0:T(8,128)} copy(f32[27,4,8,128]{3,2,1,0:T(8,128)} %get-tuple-element.12) | data formatting | bytes 884736
  33.5 0.0 copy-done
  33.5 0.6 %copy.11 = f32[4,8,128]{2,1,0:T(8,128)} copy(f32[4,8,128]{2,1,0:T(8,128)S(1)} %bitcast.7) | data formatting | bytes 32768
Async XLA Ops:
  30.4 0.7 %copy-start.1 = (f32[3,128]{1,0:T(4,128)S(1)}, f32[3,128]{1,0:T(4,128)}, u32[]{:S(2)}) copy-start(f32[3,128]{1,0:T(4,128)} %get-tuple-element.8) | copy-start | bytes 4612
  31.7 1.8 %copy-start = (f32[32,128]{1,0:T(8,128)S(1)}, f32[32,128]{1,0:T(8,128)}, u32[]{:S(2)}) copy-start(f32[32,128]{1,0:T(8,128)} %get-tuple-element.7) | copy-start | bytes 49156

commit v2 on v1

--- a/solution.py
+++ b/solution.py
@@ -42,11 +42,11 @@
 
 def kernel(
     steps, nx, ny, nz, ngx, ngy,
-    idx_ref, ck_hbm, solid_hbm, omega_hbm, adj_hbm,
-    out_ref, sens_ref, growth_ref,
-    ck_ref, solid_ref, omega_ref, adj_ref,
-    fld, ysend, yrecv, fval, mom, terms, acc_ref, line_y, line_x, own_y, own_x,
-    local_sem, send_sem, recv_sem, ysum_send, ysum_recv, xsum_send, xsum_recv,
+    idx_hbm, ck_hbm, solid_hbm, omega_hbm, adj_hbm,
+    raw_hbm, terms_hbm, sums_hbm,
+    idx_ref, ck_ref, solid_ref, omega_ref, adj_ref,
+    fld, ysend, yrecv, fval, mom, terms, acc_ref, line, own,
+    local_sem, send_sem, recv_sem, sum_send, sum_recv,
 ):
     gx, gy = lax.axis_index("gx"), lax.axis_index("gy")
     plane = 27 * ny
@@ -60,21 +60,28 @@
     loads = [
         pltpu.make_async_copy(src, dst, local_sem.at[n])
         for n, (src, dst) in enumerate(
-            ((adj_hbm, adj_ref), (ck_hbm, ck_ref), (solid_hbm, solid_ref), (omega_hbm, omega_ref))
+            (
+                (adj_hbm, adj_ref),
+                (ck_hbm, ck_ref),
+                (solid_hbm, solid_ref),
+                (omega_hbm, omega_ref),
+                (idx_hbm, idx_ref),
+            )
         )
     ]
+    barrier = pltpu.get_barrier_semaphore()
+    here = gx * ngy + gy
+    every = ngx * ngy
+    others = []
+    for k in range(1, every):
+        there = lax.rem(here + k, every)
+        others.append((there // ngy, lax.rem(there, ngy)))
+    greeted = others
+    for device in greeted:
+        pl.semaphore_signal(barrier, inc=1, device_id=device, device_id_type=MESH)
+
     for copy in loads:
         copy.start()
-
-    barrier = pltpu.get_barrier_semaphore()
-    greeted = (
-        [(gxs(k), gy) for k in range(1, ngx)]
-        + [(gx, gys(k)) for k in range(1, ngy)]
-        + [(gxs(a), gys(b)) for a in (-1, 1) for b in (-1, 1)]
-    )
-    for device in greeted:
-        pl.semaphore_signal(barrier, inc=1, device_id=device, device_id_type=MESH)
-
     loads[0].wait()
     for x in range(nx):
         for i in range(27):
@@ -201,7 +208,11 @@
     for s in range(steps):
         moving = copies(s)
         sent += moving
-        for copy in moving:
+        for copy in moving[:2]:
+            copy.start()
+        if s > 0:
+            pack(s)
+        for copy in moving[2:]:
             copy.start()
         if s == 0:
             for copy in loads[1:]:
@@ -213,57 +224,98 @@
         for copy in moving[:2] + moving[4:]:
             copy.wait_recv()
         lax.fori_loop(0, 2, lambda t, _, s=s: (step_plane(s, t * (nx - 1)), 0)[1], 0)
-        if s + 1 < steps:
-            pack(s + 1)
+
+    for x in range(nx):
+        for i in range(27):
+            adj_ref[i, x] = fld[steps, pl.ds((x + 1) * plane + i * ny, ny), :]
+    outs = [
+        pltpu.make_async_copy(adj_ref, raw_hbm, local_sem.at[0]),
+        pltpu.make_async_copy(terms, terms_hbm, local_sem.at[1]),
+    ]
 
     lane = lax.broadcasted_iota(jnp.int32, (1, nz), 1)
     row = jnp.zeros((1, nz), jnp.float32)
     for s in range(steps):
         value = jnp.sum(jnp.sum(acc_ref[s], axis=0, keepdims=True), axis=1, keepdims=True)
         row = row + jnp.where(lane == s, value, 0.0)
-
-    def spread(row, own, line, me, count, send, recv, place):
-        own[0] = row
-        copies = [
-            pltpu.make_async_remote_copy(
-                src_ref=own.at[0],
-                dst_ref=line.at[k - 1],
-                send_sem=send.at[k - 1],
-                recv_sem=recv.at[k - 1],
-                device_id=place(k),
-                device_id_type=MESH,
-            )
-            for k in range(1, count)
-        ]
-        for copy in copies:
-            copy.start()
-        for copy in copies:
-            copy.wait_recv()
-        for k in range(count - 1):
-            row = row + line[k]
-        return row, copies
-
-    row, more = spread(row, own_y, line_y, gy, ngy, ysum_send, ysum_recv, lambda k: (gx, gys(k)))
-    sent += more
-    row, more = spread(row, own_x, line_x, gx, ngx, xsum_send, xsum_recv, lambda k: (gxs(k), gy))
-    sent += more
-
-    inverse = jnp.ones((1, nz), jnp.float32)
-    sens = jnp.zeros((nx * ny, nz), jnp.float32)
-    count = float(27 * nx * ny * nz * ngx * ngy)
-    for s in range(steps):
-        sens = sens + terms[s] * inverse
-        total = jnp.sum(jnp.where(lane == s, row, 0.0), axis=1, keepdims=True)
-        total = jnp.broadcast_to(total, (1, nz))
-        factor = jnp.sqrt(total * (inverse * inverse) * (1.0 / count) + 1e-06)
-        inverse = inverse / factor
-        growth_ref[pl.ds(s, 1), :] = factor
-    sens_ref[...] = sens
-    for x in range(nx):
-        for i in range(27):
-            out_ref[i, x] = fld[steps, pl.ds((x + 1) * plane + i * ny, ny), :] * inverse
+    own[0] = row
+    moving = [
+        pltpu.make_async_remote_copy(
+            src_ref=own.at[0],
+            dst_ref=line.at[here],
+            send_sem=sum_send.at[k],
+            recv_sem=sum_recv.at[k],
+            device_id=device,
+            device_id_type=MESH,
+        )
+        for k, device in enumerate(others)
+    ]
+    for copy in moving:
+        copy.start()
+    sent += moving
+    for copy in outs:
+        copy.start()
+    for copy in moving:
+        copy.wait_recv()
+    line[here] = row
+    row = line[0]
+    for k in range(1, every):
+        row = row + line[k]
+    own[1] = row
+    last_copy = pltpu.make_async_copy(own.at[1], sums_hbm, local_sem.at[2])
+    last_copy.start()
     for copy in sent:
         copy.wait_send()
+    for copy in outs:
+        copy.wait()
+    last_copy.wait()
+
+
+def finish(
+    steps, entries, parts,
+    raw_hbm, terms_hbm, sums_hbm, out_hbm, sens_hbm, growth_ref,
+    raw, terms, sums, sens, load_sem, store_sem,
+):
+    cut = raw.shape[0] // parts
+    small = [
+        pltpu.make_async_copy(sums_hbm, sums, load_sem.at[parts]),
+        pltpu.make_async_copy(terms_hbm, terms, load_sem.at[parts + 1]),
+    ]
+    pieces = [pl.ds(k * cut, cut) for k in range(parts)]
+    loads = [
+        pltpu.make_async_copy(raw_hbm.at[piece], raw.at[piece], load_sem.at[k])
+        for k, piece in enumerate(pieces)
+    ]
+    for copy in small + loads:
+        copy.start()
+    stores = [
+        pltpu.make_async_copy(raw.at[piece], out_hbm.at[piece], store_sem.at[k])
+        for k, piece in enumerate(pieces)
+    ]
+    stores.append(pltpu.make_async_copy(sens, sens_hbm, store_sem.at[parts]))
+    for copy in small:
+        copy.wait()
+    row = sums[...]
+    lane = lax.broadcasted_iota(jnp.int32, row.shape, 1)
+    inverse = jnp.ones(row.shape, jnp.float32)
+    total = jnp.zeros(sens.shape, jnp.float32)
+    factors = []
+    for s in range(steps):
+        total = total + terms[s] * inverse
+        value = jnp.sum(jnp.where(lane == s, row, 0.0), axis=1, keepdims=True)
+        value = jnp.broadcast_to(value, row.shape)
+        factors.append(jnp.sqrt(value * (inverse * inverse) * (1.0 / entries) + 1e-06))
+        inverse = inverse / factors[-1]
+    sens[...] = total
+    stores[parts].start()
+    for k, piece in enumerate(pieces):
+        loads[k].wait()
+        raw[piece] = raw[piece] * inverse.reshape((1, 1, 1, -1))
+        stores[k].start()
+    for s in range(steps):
+        growth_ref[s] = factors[s][0, 0]
+    for copy in stores:
+        copy.wait()
 
 
 def body(checkpoints, step_ckpt, solid_mask, omega, adjoint_init):
@@ -272,19 +324,20 @@
     ngx, ngy = lax.axis_size("gx"), lax.axis_size("gy")
     f32 = jnp.float32
     hbm = pl.BlockSpec(memory_space=pltpu.HBM)
-    vmem = pl.BlockSpec(memory_space=pltpu.VMEM)
     dma = pltpu.SemaphoreType.DMA
     rows = (nx + 2) * 27 * ny
-    out, sens, growth = pl.pallas_call(
+    others = ngx * ngy - 1
+    raw, terms, sums = pl.pallas_call(
         functools.partial(kernel, steps, nx, ny, nz, ngx, ngy),
         out_shape=(
             jax.ShapeDtypeStruct(adjoint_init.shape, f32),
-            jax.ShapeDtypeStruct((nx * ny, nz), f32),
-            jax.ShapeDtypeStruct((steps, nz), f32),
+            jax.ShapeDtypeStruct((steps, nx * ny, nz), f32),
+            jax.ShapeDtypeStruct((1, nz), f32),
         ),
-        in_specs=[pl.BlockSpec(memory_space=pltpu.SMEM), hbm, hbm, hbm, hbm],
-        out_specs=(vmem, vmem, vmem),
+        in_specs=[hbm, hbm, hbm, hbm, hbm],
+        out_specs=(hbm, hbm, hbm),
         scratch_shapes=[
+            pltpu.SMEM((steps,), jnp.int32),
             pltpu.VMEM((nck, 27, nx * ny, nz), checkpoints.dtype),
             pltpu.VMEM((nx * ny, nz), jnp.int32),
             pltpu.VMEM((nx * ny, nz), f32),
@@ -296,17 +349,13 @@
             pltpu.VMEM((steps, 4, nx * ny, nz), f32),
             pltpu.VMEM((steps, nx * ny, nz), f32),
             pltpu.VMEM((steps, ny, nz), f32),
-            pltpu.VMEM((max(ngy - 1, 1), 1, nz), f32),
-            pltpu.VMEM((max(ngx - 1, 1), 1, nz), f32),
-            pltpu.VMEM((1, 1, nz), f32),
-            pltpu.VMEM((1, 1, nz), f32),
-            dma((4,)),
+            pltpu.VMEM((others + 1, 1, nz), f32),
+            pltpu.VMEM((2, 1, nz), f32),
+            dma((5,)),
             dma((steps, 8)),
             dma((steps, 8)),
-            dma((max(ngy - 1, 1),)),
-            dma((max(ngy - 1, 1),)),
-            dma((max(ngx - 1, 1),)),
-            dma((max(ngx - 1, 1),)),
+            dma((others,)),
+            dma((others,)),
         ],
         compiler_params=pltpu.CompilerParams(
             collective_id=0, has_side_effects=True, vmem_limit_bytes=60 * 1024 * 1024
@@ -319,7 +368,28 @@
         omega.reshape(nx * ny, nz),
         adjoint_init,
     )
-    return out, sens.reshape(omega.shape), growth[:, 0]
+    parts = 3
+    out, sens, growth = pl.pallas_call(
+        functools.partial(finish, steps, float(adjoint_init.size * ngx * ngy), parts),
+        out_shape=(
+            jax.ShapeDtypeStruct(adjoint_init.shape, f32),
+            jax.ShapeDtypeStruct((nx * ny, nz), f32),
+            jax.ShapeDtypeStruct((steps,), f32),
+        ),
+        in_specs=[hbm, hbm, hbm],
+        out_specs=(hbm, hbm, pl.BlockSpec(memory_space=pltpu.SMEM)),
+        scratch_shapes=[
+            pltpu.VMEM(adjoint_init.shape, f32),
+            pltpu.VMEM((steps, nx * ny, nz), f32),
+            pltpu.VMEM((1, nz), f32),
+            pltpu.VMEM((nx * ny, nz), f32),
+            dma((parts + 2,)),
+            dma((parts + 1,)),
+        ],
+        compiler_params=pltpu.CompilerParams(vmem_limit_bytes=60 * 1024 * 1024),
+        cost_estimate=pl.CostEstimate(flops=10**5, bytes_accessed=10**6, transcendentals=0),
+    )(raw, terms, sums)
+    return out, sens.reshape(omega.shape), growth
 
 
 def solution(mesh):

time: 34.3 us -> 31.6 us (0.921)
  local copies, waits for them, and re-layouts: 3.72 us -> 0 us
  Pallas kernels: 29.7 us -> 30.8 us
    unnamed x6 -> x0, local copies, waits for them, and re-layouts: 3.1 us -> none
    pallas_call x0 -> x1, Pallas kernels: none -> 2.35 us  [body(): pl.pallas_call(functools.partial(finish, steps, float(adjoint_init.size *...]
    pallas_call x1, Pallas kernels: 29.7 us -> 28.4 us  [body(): pl.pallas_call(functools.partial(kernel, steps, nx, ny, nz, ngx, ngy), ou...]
    slice x1 -> x0, local copies, waits for them, and re-layouts: 0.63 us -> none  [body(): return (out, sens.reshape(omega.shape), growth[:, 0])]
where the time goes in v2:
time: 31.6 us; the launch traced here: 31.4 us
  Pallas kernels  30.8 us (97%)
  between operations  0.64 us (2%)
    pallas_call x1, Pallas kernels, body(): pl.pallas_call(functools.partial(kernel, steps, nx, ny, nz, ngx, ngy), ou...  28.4 us
    pallas_call x1, Pallas kernels, body(): pl.pallas_call(functools.partial(finish, steps, float(adjoint_init.size *...  2.35 us

profile of v2, /device:TPU:0, one launch (start us, length us, event | category | flops | bytes accessed | tf_op | source)
XLA Modules:
  0.0 31.4 jit_solution(13983551781197536033)
XLA Ops:
  0.6 28.4 %shard_map.76 = (f32[27,4,8,128]{3,2,1,0:T(8,128)}, f32[3,32,128]{2,1,0:T(8,128)}, f32[1,128]{1,0:T(1,128)}) custom-call(s32[3]{0:T(128)} %idx_hbm.1, bf16[4,27,32,128]{3,2,1,0:T(8,128)(2,1)} %bitcast.4, s32[32,128]{1,0:T(8,128)} %bitcast.5, f32[32,128]{1,0:T(8,128)} %bitcast.6, f32[27,4,8,128]{3,2,1,0:T(8,128)} %adj_hbm.1), custom_call_target="tpu_custom_call" | custom-call | flops 10000000 | bytes 2000000 | tf_op jit(solution)/shard_map/pallas_call | solution.py:330
  29.1 2.4 %shard_map.77 = (f32[27,4,8,128]{3,2,1,0:T(8,128)}, f32[32,128]{1,0:T(8,128)}, f32[3]{0:T(128)}) custom-call(f32[27,4,8,128]{3,2,1,0:T(8,128)} %get-tuple-element.9.raw_hbm, f32[3,32,128]{2,1,0:T(8,128)} %get-tuple-element.10.terms_hbm, f32[1,128]{1,0:T(1,128)} %get-tuple-element.11.sums_hbm), custom_call_target="tpu_custom_call" | custom-call | flops 100000 | bytes 1000000 | tf_op jit(solution)/shard_map/pallas_call | solution.py:372

commit v3 on v2

--- a/solution.py
+++ b/solution.py
@@ -243,20 +243,19 @@
         pltpu.make_async_remote_copy(
             src_ref=own.at[0],
             dst_ref=line.at[here],
-            send_sem=sum_send.at[k],
-            recv_sem=sum_recv.at[k],
+            send_sem=sum_send,
+            recv_sem=sum_recv,
             device_id=device,
             device_id_type=MESH,
         )
-        for k, device in enumerate(others)
+        for device in others
     ]
     for copy in moving:
         copy.start()
-    sent += moving
     for copy in outs:
         copy.start()
-    for copy in moving:
-        copy.wait_recv()
+    bulk = line.at[pl.ds(0, every - 1)]
+    pltpu.make_async_copy(bulk, bulk, sum_recv).wait()
     line[here] = row
     row = line[0]
     for k in range(1, every):
@@ -266,6 +265,7 @@
     last_copy.start()
     for copy in sent:
         copy.wait_send()
+    pltpu.make_async_copy(bulk, bulk, sum_send).wait()
     for copy in outs:
         copy.wait()
     last_copy.wait()
@@ -354,8 +354,8 @@
             dma((5,)),
             dma((steps, 8)),
             dma((steps, 8)),
-            dma((others,)),
-            dma((others,)),
+            dma,
+            dma,
         ],
         compiler_params=pltpu.CompilerParams(
             collective_id=0, has_side_effects=True, vmem_limit_bytes=60 * 1024 * 1024

time: 31.6 us -> 31 us (0.981)
  Pallas kernels: 30.8 us -> 30.2 us
    pallas_call x1, Pallas kernels: 28.4 us -> 27.8 us  [body(): pl.pallas_call(functools.partial(kernel, steps, nx, ny, nz, ngx, ngy), ou...]
where the time goes in v3:
time: 31 us; the launch traced here: 30.8 us
  Pallas kernels  30.2 us (97%)
  between operations  0.64 us (2%)
    pallas_call x1, Pallas kernels, body(): pl.pallas_call(functools.partial(kernel, steps, nx, ny, nz, ngx, ngy), ou...  27.8 us
    pallas_call x1, Pallas kernels, body(): pl.pallas_call(functools.partial(finish, steps, float(adjoint_init.size *...  2.35 us

profile of v3, /device:TPU:0, one launch (start us, length us, event | category | flops | bytes accessed | tf_op | source)
XLA Modules:
  0.0 30.8 jit_solution(10938283692455406228)
XLA Ops:
  0.6 27.8 %shard_map.76 = (f32[27,4,8,128]{3,2,1,0:T(8,128)}, f32[3,32,128]{2,1,0:T(8,128)}, f32[1,128]{1,0:T(1,128)}) custom-call(s32[3]{0:T(128)} %idx_hbm.1, bf16[4,27,32,128]{3,2,1,0:T(8,128)(2,1)} %bitcast.4, s32[32,128]{1,0:T(8,128)} %bitcast.5, f32[32,128]{1,0:T(8,128)} %bitcast.6, f32[27,4,8,128]{3,2,1,0:T(8,128)} %adj_hbm.1), custom_call_target="tpu_custom_call" | custom-call | flops 10000000 | bytes 2000000 | tf_op jit(solution)/shard_map/pallas_call | solution.py:330
  28.5 2.4 %shard_map.77 = (f32[27,4,8,128]{3,2,1,0:T(8,128)}, f32[32,128]{1,0:T(8,128)}, f32[3]{0:T(128)}) custom-call(f32[27,4,8,128]{3,2,1,0:T(8,128)} %get-tuple-element.9.raw_hbm, f32[3,32,128]{2,1,0:T(8,128)} %get-tuple-element.10.terms_hbm, f32[1,128]{1,0:T(1,128)} %get-tuple-element.11.sums_hbm), custom_call_target="tpu_custom_call" | custom-call | flops 100000 | bytes 1000000 | tf_op jit(solution)/shard_map/pallas_call | solution.py:372
